TPU v7x, 32 devices: a whole 2x2x4 slice. The times are simulated.
32 devices in a mesh: row: 2 (over core), col: 16 (over z, y, x).
Axes of the slice: x: 2, y: 2, z: 4, core: 2. Of those that a mesh axis runs over, the one named last changes fastest.
Arguments:
- object_re: float32 [512, 4096], P('row', 'col'), may hold values from -6 to 6
- object_im: float32 [512, 4096], P('row', 'col'), may hold values from -6 to 6
- probe_re: float32 [256, 256], replicated, may hold values from -4 to 4
- probe_im: float32 [256, 256], replicated, may hold values from -4 to 4
- intensity: float32 [2, 16, 4, 256, 256], P('row', 'col'), may hold values from 0.05 to 4
- offsets: int32 [2, 16, 4, 2], P('row', 'col'), may hold values from 48 to 208
- counts: int32 [2, 16], P('row', 'col'), may hold values from 2 to 4
Outputs:
- final_re: float32 [512, 4096], P('row', 'col')
- final_im: float32 [512, 4096], P('row', 'col')
All inputs are finite; a program needn't handle non-finite values.
Results may differ from a plain program's by a relative error of at most 0.00024.
Values sent between devices are 32-bit elements; how exact they have to be, the bound alone decides.
A program may use at most 64 MiB of HBM per device.

v0:
```python
import functools
import math

import jax
import jax.numpy as jnp
import numpy as np
from jax import lax
from jax.experimental import pallas as pl
from jax.experimental.pallas import tpu as pltpu
from jax.sharding import PartitionSpec as P

ITERS = 2
smoothing = 0.01
step_size = 0.25
MESH = pl.DeviceIdType.MESH


def split_tables(length):
    half = length // 2
    n = np.arange(half)
    tables = []
    for odd in (0, 1):
        phase = (2 * n[:, None] + odd) * n[None, :] % length
        angle = phase * (-2.0 * math.pi / length)
        re, im = np.cos(angle) / math.sqrt(length), np.sin(angle) / math.sqrt(length)
        tables.append(np.block([[re, -im], [im, re]]))
    bf16 = jnp.bfloat16
    left, right = [], []
    for table in (tables[0], tables[1], tables[0].T, tables[1].T):
        high = table.astype(np.float32).astype(bf16)
        low = (table - high.astype(np.float64)).astype(np.float32).astype(bf16)
        left.append(np.concatenate([high, high, low], axis=1))
        right.append(np.concatenate([high, high, low], axis=0))
    return np.stack(left), np.stack(right)


def terms(x, axis):
    high = x.astype(jnp.bfloat16)
    low = (x - high.astype(jnp.float32)).astype(jnp.bfloat16)
    return jnp.concatenate([high, low, high], axis=axis)


def mul_left(table, x):
    return jnp.dot(table, terms(x, 0), preferred_element_type=jnp.float32)


def mul_right(x, table):
    return jnp.dot(terms(x, 1), table, preferred_element_type=jnp.float32)


def kernel(
    rows, cols, offsets, counts, object_re, object_im, probe_re, probe_im, intensity, left, right,
    out_re, out_im, ext, grad, probes, roots, picked, turned, from_rows, from_cols, send, recv,
):
    width = probe_re.shape[0]
    half = width // 2
    full = 2 * width
    slots = intensity.shape[0]
    reach = half - half // 2 + half // 8
    inner = slice(half, half + width)
    lo, hi = half - reach, half + width + reach
    row, col = lax.axis_index("row"), lax.axis_index("col")
    there = {
        "up": (row > 0, {"row": row - 1}), "down": (row < rows - 1, {"row": row + 1}),
        "left": (col > 0, {"col": col - 1}), "right": (col < cols - 1, {"col": col + 1}),
    }
    opposite = {"up": "down", "down": "up", "left": "right", "right": "left"}

    ext[...] = jnp.zeros_like(ext)
    ext[0, inner, inner] = object_re[...].T
    ext[1, inner, inner] = object_im[...].T

    barrier = pltpu.get_barrier_semaphore()
    for exists, device in there.values():
        @pl.when(exists)
        def _(device=device):
            pl.semaphore_signal(barrier, inc=1, device_id=device, device_id_type=MESH)
    pl.semaphore_wait(barrier, sum(exists.astype(jnp.int32) for exists, _ in there.values()))

    serial = [0]

    class Send:
        def __init__(self, side, src, dst):
            exists, device = there[side]
            self.out, self.arrives = exists, there[opposite[side]][0]
            self.copy = pltpu.make_async_remote_copy(
                src_ref=src, dst_ref=dst, send_sem=send.at[serial[0]], recv_sem=recv.at[serial[0]],
                device_id=device, device_id_type=MESH,
            )
            serial[0] += 1
            pl.when(self.out)(self.copy.start)

        def received(self):
            pl.when(self.arrives)(self.copy.wait_recv)

        def sent(self):
            pl.when(self.out)(self.copy.wait_send)

    def finish(copies):
        for copy in copies:
            copy.received()
        for copy in copies:
            copy.sent()

    def send_rows(first, last):
        cells = slice(first, last)
        return [
            Send("up", ext.at[:, cells, half : 2 * half], ext.at[:, cells, half + width : full]),
            Send("down", ext.at[:, cells, width : width + half], ext.at[:, cells, 0:half]),
        ]

    sideways = [
        Send("left", ext.at[:, half : half + reach, inner], ext.at[:, half + width : hi, inner]),
        Send("right", ext.at[:, half + width - reach : half + width, inner], ext.at[:, lo:half, inner]),
    ]
    upright = send_rows(half, half + width)

    for p in range(slots):
        down_by = lax.rem(offsets[p, 0] + half, width)
        along_by = lax.rem(offsets[p, 1] + half, width)
        for part, source in enumerate((probe_re, probe_im)):
            moved = pltpu.roll(source[...].T, along_by, 0)
            probes[p, part] = pltpu.roll(moved, down_by, 1)
        for other in (0, 1):
            block = slice(other * half, other * half + half)
            picked[other] = intensity[p, :, block]
        for odd in (0, 1):
            for other in (0, 1):
                block = slice(other * half, other * half + half)
                turned[block, :] = picked[other, pl.ds(odd, half, stride=2), :].T
            for v in (0, 1):
                roots[p, v * half : v * half + half, odd * half : odd * half + half] = jnp.sqrt(
                    turned[pl.ds(v, half, stride=2), :]
                )

    finish(sideways)
    corners = send_rows(lo, half) + send_rows(half + width, hi)
    finish(upright)
    finish(corners)

    across = lax.broadcasted_iota(jnp.int32, (half, full), 0)
    along = lax.broadcasted_iota(jnp.int32, (width, half), 1)

    def own_cells(index, start, cells):
        return cells + half < start + width if index == 0 else cells >= start

    def visit(p):
        a, b = p // 2, p % 2
        top, start = offsets[p, 0] - half, offsets[p, 1] - half
        own_c = own_cells(b, start, across)
        own_r = own_cells(a, top, along)
        used = p < counts[0]

        def patch(part):
            first, second = ext[part, half:width, :], ext[part, width : width + half, :]
            if b == 0:
                second = jnp.where(own_c, second, ext[part, 0:half, :])
            else:
                first = jnp.where(own_c, first, ext[part, half + width : full, :])
            both = jnp.concatenate([first, second], axis=0)
            first, second = both[:, half:width], both[:, width : width + half]
            if a == 0:
                second = jnp.where(own_r, second, both[:, 0:half])
            else:
                first = jnp.where(own_r, first, both[:, half + width : full])
            return jnp.concatenate([first, second], axis=1)

        def place(part, term):
            if a == 0:
                pieces = [jnp.where(own_r, 0.0, term[:, half:]), term[:, :half], jnp.where(own_r, term[:, half:], 0.0)]
                cells = slice(0, half + width)
            else:
                pieces = [jnp.where(own_r, term[:, :half], 0.0), term[:, half:], jnp.where(own_r, 0.0, term[:, :half])]
                cells = slice(half, full)
            term = jnp.concatenate(pieces, axis=1)
            own = own_c[:, : term.shape[1]]
            first, second = term[:half], term[half:]
            if b == 0:
                grad[part, 0:half, cells] += jnp.where(own, 0.0, second)
                second = jnp.where(own, second, 0.0)
            else:
                grad[part, half + width : full, cells] += jnp.where(own, 0.0, first)
                first = jnp.where(own, first, 0.0)
            grad[part, half:width, cells] += first
            grad[part, width : width + half, cells] += second

        cell_re, cell_im = patch(0), patch(1)
        probe_r, probe_i = probes[p, 0], probes[p, 1]
        re = cell_re * probe_r - cell_im * probe_i
        im = cell_re * probe_i + cell_im * probe_r
        even = mul_left(left[0], jnp.concatenate([re[:half] + re[half:], im[:half] + im[half:]], axis=0))
        odd = mul_left(left[1], jnp.concatenate([re[:half] - re[half:], im[:half] - im[half:]], axis=0))
        re = jnp.concatenate([even[:half], odd[:half]], axis=0)
        im = jnp.concatenate([even[half:], odd[half:]], axis=0)
        far = [
            mul_right(jnp.concatenate([re[:, :half] + re[:, half:], im[:, :half] + im[:, half:]], axis=1), right[2]),
            mul_right(jnp.concatenate([re[:, :half] - re[:, half:], im[:, :half] - im[:, half:]], axis=1), right[3]),
        ]
        back = []
        for which, wave in enumerate(far):
            re, im = wave[:, :half], wave[:, half:]
            root = roots[p, :, which * half : which * half + half]
            factor = 1.0 - root * lax.rsqrt(re * re + im * im + smoothing)
            chi = jnp.concatenate([re * factor, im * factor], axis=1)
            back.append(mul_right(chi, right[which]))
        low, high = back[0] + back[1], back[0] - back[1]
        re = jnp.concatenate([low[:, :half], high[:, :half]], axis=1)
        im = jnp.concatenate([low[:, half:], high[:, half:]], axis=1)
        even = mul_left(left[2], jnp.concatenate([re[:half], im[:half]], axis=0))
        odd = mul_left(left[3], jnp.concatenate([re[half:], im[half:]], axis=0))
        low, high = even + odd, even - odd
        re = jnp.concatenate([low[:half], high[:half]], axis=0)
        im = jnp.concatenate([low[half:], high[half:]], axis=0)
        place(0, jnp.where(used, re * probe_r + im * probe_i, 0.0))
        place(1, jnp.where(used, im * probe_r - re * probe_i, 0.0))

    for sweep in range(ITERS):
        grad[...] = jnp.zeros_like(grad)
        for p in range(slots):
            visit(p)

        cells = slice(lo, hi)
        copies = [
            Send("up", grad.at[:, cells, 0:half], from_rows.at[sweep, 1]),
            Send("down", grad.at[:, cells, half + width : full], from_rows.at[sweep, 0]),
        ]
        finish(copies)
        pl.when(there["up"][0])(functools.partial(add, grad, cells, slice(half, 2 * half), from_rows.at[sweep, 0]))
        pl.when(there["down"][0])(functools.partial(add, grad, cells, slice(width, width + half), from_rows.at[sweep, 1]))

        more = sweep < ITERS - 1
        kept = reach if more else 0
        wide = reach + kept
        copies = [
            Send("left", grad.at[:, lo : half + kept, inner], from_cols.at[sweep, 1, :, 0:wide]),
            Send("right", grad.at[:, half + width - kept : hi, inner], from_cols.at[sweep, 0, :, 0:wide]),
        ]
        finish(copies)
        pl.when(there["left"][0])(
            functools.partial(add, grad, slice(half - kept, half + reach), inner, from_cols.at[sweep, 0, :, 0:wide])
        )
        pl.when(there["right"][0])(
            functools.partial(
                add, grad, slice(half + width - reach, half + width + kept), inner, from_cols.at[sweep, 1, :, 0:wide]
            )
        )
        if more:
            new = ext[:, lo:hi, inner] - step_size * grad[:, lo:hi, inner]
            ext[:, half : half + width, inner] = new[:, reach : reach + width]

            @pl.when(there["left"][0])
            def _():
                ext[:, lo:half, inner] = new[:, :reach]

            @pl.when(there["right"][0])
            def _():
                ext[:, half + width : hi, inner] = new[:, reach + width :]

            finish(send_rows(lo, hi))
    out_re[...] = (ext[0, inner, inner] - step_size * grad[0, inner, inner]).T
    out_im[...] = (ext[1, inner, inner] - step_size * grad[1, inner, inner]).T


def add(total, rows, cols, term):
    total[:, rows, cols] += term[...]


def shards(rows, cols, object_re, object_im, probe_re, probe_im, intensity, offsets, counts):
    width = probe_re.shape[0]
    half = width // 2
    reach = half - half // 2 + half // 8
    slots = intensity.shape[2]
    left, right = split_tables(width)
    f32 = jnp.float32
    vmem = pl.BlockSpec(memory_space=pltpu.VMEM)
    smem = pl.BlockSpec(memory_space=pltpu.SMEM)
    tile = jax.ShapeDtypeStruct(object_re.shape, f32)
    return pl.pallas_call(
        functools.partial(kernel, rows, cols),
        out_shape=(tile, tile),
        in_specs=[smem, smem] + [vmem] * 7,
        out_specs=(vmem, vmem),
        scratch_shapes=[
            pltpu.VMEM((2, 2 * width, 2 * width), f32),
            pltpu.VMEM((2, 2 * width, 2 * width), f32),
            pltpu.VMEM((slots, 2, width, width), f32),
            pltpu.VMEM((slots, width, width), f32),
            pltpu.VMEM((2, width, half), f32),
            pltpu.VMEM((width, half), f32),
            pltpu.VMEM((ITERS, 2, 2, width + 2 * reach, half), f32),
            pltpu.VMEM((ITERS, 2, 2, 2 * reach, width), f32),
            pltpu.SemaphoreType.DMA((24,)),
            pltpu.SemaphoreType.DMA((24,)),
        ],
        compiler_params=pltpu.CompilerParams(
            collective_id=0, has_side_effects=True, vmem_limit_bytes=56 * 1024 * 1024
        ),
    )(
        offsets[0, 0], counts[0], object_re, object_im, probe_re, probe_im, intensity[0, 0],
        jnp.asarray(left), jnp.asarray(right),
    )


def solution(mesh):
    return jax.shard_map(
        functools.partial(shards, mesh.shape["row"], mesh.shape["col"]),
        mesh=mesh,
        in_specs=(
            P("row", "col"),
            P("row", "col"),
            P(),
            P(),
            P("row", "col", None, None, None),
            P("row", "col", None, None),
            P("row", "col"),
        ),
        out_specs=(P("row", "col"), P("row", "col")),
        check_vma=False,
    )
```

profile of v0, /device:TPU:13, one launch (start us, length us, event | category | flops | bytes accessed | tf_op | source)
XLA Modules:
  0.0 62.8 jit_solution(6808885225486716618)
XLA Ops:
  1.3 1.3 %copy.11.offsets = s32[4,2]{1,0:T(4,128)} copy(s32[4,2]{0,1:T(2,128)} %bitcast.5) | data formatting | bytes 64 | tf_op jit(solution)/shard_map/squeeze | solution.py:299
  2.6 56.8 %shard_map.104 = (f32[256,256]{1,0:T(8,128)}, f32[256,256]{1,0:T(8,128)}) custom-call(s32[4,2]{1,0:T(4,128)} %copy.11.offsets, s32[1]{0:T(128)} %bitcast.3.counts, f32[256,256]{1,0:T(8,128)} %object_re.1, f32[256,256]{1,0:T(8,128)} %object_im.1, f32[256,256]{1,0:T(8,128)} %probe_re.1, f32[256,256]{1,0:T(8,128)} %probe_im.1, f32[4,256,256]{2,1,0:T(8,128)} %bitcast.4, ...), custom_call_target="tpu_custom_call" | custom-call | tf_op jit(solution)/shard_map/pallas_call | solution.py:278
  59.4 1.7 %copy.15 = f32[256,256]{1,0:T(8,128)} copy(f32[256,256]{1,0:T(8,128)} %get-tuple-element.4) | data formatting | bytes 524288
  61.1 1.7 %copy.16 = f32[256,256]{1,0:T(8,128)} copy(f32[256,256]{1,0:T(8,128)} %get-tuple-element.5) | data formatting | bytes 524288
where the time goes:
time: 63 us; the launch traced here: 62.8 us
  Pallas kernels  56.8 us (90%)
  local copies, waits for them, and re-layouts  4.68 us (7%)
  between operations  1.29 us (2%)
    pallas_call x1, Pallas kernels, shards(): pl.pallas_call(functools.partial(kernel, rows, cols), out_shape=(tile, ti...  56.8 us
    unnamed x2, local copies, waits for them, and re-layouts  3.34 us
    squeeze x1, local copies, waits for them, and re-layouts, shards(): offsets[0, 0]  1.34 us

commit v1 on v0

--- a/solution.py
+++ b/solution.py
@@ -67,6 +67,9 @@
     opposite = {"up": "down", "down": "up", "left": "right", "right": "left"}
 
     ext[...] = jnp.zeros_like(ext)
+    from_rows[...] = jnp.zeros_like(from_rows)
+    from_cols[...] = jnp.zeros_like(from_cols)
+    grad[...] = jnp.zeros_like(grad)
     ext[0, inner, inner] = object_re[...].T
     ext[1, inner, inner] = object_im[...].T
 
@@ -109,10 +112,7 @@
             Send("down", ext.at[:, cells, width : width + half], ext.at[:, cells, 0:half]),
         ]
 
-    sideways = [
-        Send("left", ext.at[:, half : half + reach, inner], ext.at[:, half + width : hi, inner]),
-        Send("right", ext.at[:, half + width - reach : half + width, inner], ext.at[:, lo:half, inner]),
-    ]
+    rightward = Send("right", ext.at[:, half + width - reach : half + width, inner], ext.at[:, lo:half, inner])
     upright = send_rows(half, half + width)
 
     for p in range(slots):
@@ -133,10 +133,11 @@
                     turned[pl.ds(v, half, stride=2), :]
                 )
 
-    finish(sideways)
-    corners = send_rows(lo, half) + send_rows(half + width, hi)
-    finish(upright)
-    finish(corners)
+    rightward.sent()
+    leftward = Send("left", ext.at[:, half : half + reach, inner], ext.at[:, half + width : hi, inner])
+    rightward.received()
+    corners = send_rows(lo, half)
+    finish(upright + corners)
 
     across = lax.broadcasted_iota(jnp.int32, (half, full), 0)
     along = lax.broadcasted_iota(jnp.int32, (width, half), 1)
@@ -144,7 +145,7 @@
     def own_cells(index, start, cells):
         return cells + half < start + width if index == 0 else cells >= start
 
-    def visit(p):
+    def visit(sweep, p):
         a, b = p // 2, p % 2
         top, start = offsets[p, 0] - half, offsets[p, 1] - half
         own_c = own_cells(b, start, across)
@@ -152,12 +153,13 @@
         used = p < counts[0]
 
         def patch(part):
-            first, second = ext[part, half:width, :], ext[part, width : width + half, :]
             if b == 0:
-                second = jnp.where(own_c, second, ext[part, 0:half, :])
+                mixed = jnp.where(own_c[:reach], ext[part, width : width + reach, :], ext[part, 0:reach, :])
+                pieces = [ext[part, half:width, :], mixed, ext[part, reach:half, :]]
             else:
-                first = jnp.where(own_c, first, ext[part, half + width : full, :])
-            both = jnp.concatenate([first, second], axis=0)
+                mixed = jnp.where(own_c[lo:], ext[part, half + lo : width, :], ext[part, half + width + lo : full, :])
+                pieces = [ext[part, half + width : half + width + lo, :], mixed, ext[part, width : width + half, :]]
+            both = jnp.concatenate(pieces, axis=0)
             first, second = both[:, half:width], both[:, width : width + half]
             if a == 0:
                 second = jnp.where(own_r, second, both[:, 0:half])
@@ -176,13 +178,13 @@
             own = own_c[:, : term.shape[1]]
             first, second = term[:half], term[half:]
             if b == 0:
-                grad[part, 0:half, cells] += jnp.where(own, 0.0, second)
-                second = jnp.where(own, second, 0.0)
+                grad[sweep, part, lo:half, cells] += jnp.where(own, 0.0, second)[lo:]
+                grad[sweep, part, half:width, cells] += first
+                grad[sweep, part, width : width + reach, cells] += jnp.where(own, second, 0.0)[:reach]
             else:
-                grad[part, half + width : full, cells] += jnp.where(own, 0.0, first)
-                first = jnp.where(own, first, 0.0)
-            grad[part, half:width, cells] += first
-            grad[part, width : width + half, cells] += second
+                grad[sweep, part, half + width : hi, cells] += jnp.where(own, 0.0, first)[:reach]
+                grad[sweep, part, half + lo : width, cells] += jnp.where(own, first, 0.0)[lo:]
+                grad[sweep, part, width : width + half, cells] += second
 
         cell_re, cell_im = patch(0), patch(1)
         probe_r, probe_i = probes[p, 0], probes[p, 1]
@@ -214,55 +216,89 @@
         place(0, jnp.where(used, re * probe_r + im * probe_i, 0.0))
         place(1, jnp.where(used, im * probe_r - re * probe_i, 0.0))
 
-    for sweep in range(ITERS):
-        grad[...] = jnp.zeros_like(grad)
-        for p in range(slots):
-            visit(p)
-
-        cells = slice(lo, hi)
-        copies = [
-            Send("up", grad.at[:, cells, 0:half], from_rows.at[sweep, 1]),
-            Send("down", grad.at[:, cells, half + width : full], from_rows.at[sweep, 0]),
+    def start_rows(sweep, first, last):
+        cells, slot = slice(first, last), slice(first - lo, last - lo)
+        return [
+            Send("up", grad.at[sweep, :, cells, 0:half], from_rows.at[sweep, 1, :, slot]),
+            Send("down", grad.at[sweep, :, cells, half + width : full], from_rows.at[sweep, 0, :, slot]),
         ]
+
+    def end_rows(sweep, first, last, copies):
+        cells, slot = slice(first, last), slice(first - lo, last - lo)
         finish(copies)
-        pl.when(there["up"][0])(functools.partial(add, grad, cells, slice(half, 2 * half), from_rows.at[sweep, 0]))
-        pl.when(there["down"][0])(functools.partial(add, grad, cells, slice(width, width + half), from_rows.at[sweep, 1]))
-
-        more = sweep < ITERS - 1
-        kept = reach if more else 0
-        wide = reach + kept
-        copies = [
-            Send("left", grad.at[:, lo : half + kept, inner], from_cols.at[sweep, 1, :, 0:wide]),
-            Send("right", grad.at[:, half + width - kept : hi, inner], from_cols.at[sweep, 0, :, 0:wide]),
-        ]
-        finish(copies)
-        pl.when(there["left"][0])(
-            functools.partial(add, grad, slice(half - kept, half + reach), inner, from_cols.at[sweep, 0, :, 0:wide])
-        )
-        pl.when(there["right"][0])(
-            functools.partial(
-                add, grad, slice(half + width - reach, half + width + kept), inner, from_cols.at[sweep, 1, :, 0:wide]
-            )
-        )
-        if more:
-            new = ext[:, lo:hi, inner] - step_size * grad[:, lo:hi, inner]
-            ext[:, half : half + width, inner] = new[:, reach : reach + width]
-
-            @pl.when(there["left"][0])
-            def _():
-                ext[:, lo:half, inner] = new[:, :reach]
-
-            @pl.when(there["right"][0])
-            def _():
-                ext[:, half + width : hi, inner] = new[:, reach + width :]
-
-            finish(send_rows(lo, hi))
-    out_re[...] = (ext[0, inner, inner] - step_size * grad[0, inner, inner]).T
-    out_im[...] = (ext[1, inner, inner] - step_size * grad[1, inner, inner]).T
-
-
-def add(total, rows, cols, term):
-    total[:, rows, cols] += term[...]
+        grad[sweep, :, cells, half:width] += from_rows[sweep, 0, :, slot]
+        grad[sweep, :, cells, width : width + half] += from_rows[sweep, 1, :, slot]
+
+    def start_side(sweep, side, first, last, slot):
+        landing = from_cols.at[sweep, 1 if side == "left" else 0, :, slot : slot + last - first]
+        return Send(side, grad.at[sweep, :, first:last, inner], landing)
+
+    def step(sweep, first, last, exists=None, term=None):
+        total = grad[sweep, :, first:last, inner]
+        if term is not None:
+            total = total + term
+        new = ext[:, first:last, inner] - step_size * total
+        return new if exists is None else jnp.where(exists, new, 0.0)
+
+    split_lo, split_hi = half + lo, width + reach
+    near = half + reach
+    far_in = half + width - reach
+    here_left, here_right = there["left"][0], there["right"][0]
+    left_slots = [p for p in range(slots) if p % 2 == 0]
+    right_slots = [p for p in range(slots) if p % 2 == 1]
+
+    visit(0, left_slots[0])
+    leftward.received()
+    corners = send_rows(half + width, hi)
+    for p in left_slots[1:]:
+        visit(0, p)
+    early_rows = start_rows(0, lo, split_lo)
+    finish(corners)
+    visit(0, right_slots[0])
+    end_rows(0, lo, split_lo, early_rows)
+    left_main = start_side(0, "left", lo, split_lo, 0)
+    for p in right_slots[1:]:
+        visit(0, p)
+    end_rows(0, split_lo, hi, start_rows(0, split_lo, hi))
+    left_rest = start_side(0, "left", split_lo, near, half)
+    right_rest = start_side(0, "right", far_in + half, hi, half)
+    right_main = start_side(0, "right", far_in, far_in + half, 0)
+    leftward.sent()
+    left_main.received()
+    left_rest.received()
+    right_rest.received()
+    ext[:, split_lo:near, inner] = step(0, split_lo, near, None, from_cols[0, 0, :, half : 2 * reach])
+    ext[:, near:far_in, inner] = step(0, near, far_in)
+    ext[:, far_in : half + width, inner] = step(0, far_in, half + width, None, from_cols[0, 1, :, 0:reach])
+    ext[:, half + width : hi, inner] = step(0, half + width, hi, here_right, from_cols[0, 1, :, reach : 2 * reach])
+    finish(send_rows(split_lo, hi))
+
+    visit(1, right_slots[0])
+    right_main.received()
+    ext[:, lo:half, inner] = step(0, lo, half, here_left, from_cols[0, 0, :, 0:reach])
+    ext[:, half:split_lo, inner] = step(0, half, split_lo, None, from_cols[0, 0, :, reach:half])
+    upright = send_rows(lo, split_lo)
+    for p in right_slots[1:]:
+        visit(1, p)
+    late_rows = start_rows(1, split_hi, hi)
+    finish(upright)
+    visit(1, left_slots[0])
+    end_rows(1, split_hi, hi, late_rows)
+    right_last = start_side(1, "right", half + width, hi, 0)
+    for p in left_slots[1:]:
+        visit(1, p)
+    end_rows(1, lo, split_hi, start_rows(1, lo, split_hi))
+    left_last = start_side(1, "left", lo, half, 0)
+    for part in (0, 1):
+        ext[part, near:far_in, inner] -= step_size * grad[1, part, near:far_in, inner]
+    right_last.received()
+    ext[:, half:near, inner] = step(1, half, near, None, from_cols[1, 0, :, 0:reach])
+    left_last.received()
+    ext[:, far_in : half + width, inner] = step(1, far_in, half + width, None, from_cols[1, 1, :, 0:reach])
+    out_re[...] = ext[0, inner, inner].T
+    out_im[...] = ext[1, inner, inner].T
+    for copy in (left_main, left_rest, right_rest, right_main, right_last, left_last):
+        copy.sent()
 
 
 def shards(rows, cols, object_re, object_im, probe_re, probe_im, intensity, offsets, counts):
@@ -282,15 +318,15 @@
         out_specs=(vmem, vmem),
         scratch_shapes=[
             pltpu.VMEM((2, 2 * width, 2 * width), f32),
-            pltpu.VMEM((2, 2 * width, 2 * width), f32),
+            pltpu.VMEM((ITERS, 2, 2 * width, 2 * width), f32),
             pltpu.VMEM((slots, 2, width, width), f32),
             pltpu.VMEM((slots, width, width), f32),
             pltpu.VMEM((2, width, half), f32),
             pltpu.VMEM((width, half), f32),
             pltpu.VMEM((ITERS, 2, 2, width + 2 * reach, half), f32),
             pltpu.VMEM((ITERS, 2, 2, 2 * reach, width), f32),
-            pltpu.SemaphoreType.DMA((24,)),
-            pltpu.SemaphoreType.DMA((24,)),
+            pltpu.SemaphoreType.DMA((32,)),
+            pltpu.SemaphoreType.DMA((32,)),
         ],
         compiler_params=pltpu.CompilerParams(
             collective_id=0, has_side_effects=True, vmem_limit_bytes=56 * 1024 * 1024

time: 63 us -> 56.7 us (0.900)
  the two profiles are of different devices: /device:TPU:13 before, /device:TPU:10 now
where the time goes in v1:
time: 56.7 us; the launch traced here: 56.5 us
  Pallas kernels  50.5 us (89%)
  local copies, waits for them, and re-layouts  4.68 us (8%)
  between operations  1.29 us (2%)
    pallas_call x1, Pallas kernels, shards(): pl.pallas_call(functools.partial(kernel, rows, cols), out_shape=(tile, ti...  50.5 us
    unnamed x2, local copies, waits for them, and re-layouts  3.34 us
    squeeze x1, local copies, waits for them, and re-layouts, shards(): offsets[0, 0]  1.34 us

profile of v1, /device:TPU:10, one launch (start us, length us, event | category | flops | bytes accessed | tf_op | source)
XLA Modules:
  0.0 56.5 jit_solution(1106115490643569339)
XLA Ops:
  1.3 1.3 %copy.11.offsets = s32[4,2]{1,0:T(4,128)} copy(s32[4,2]{0,1:T(2,128)} %bitcast.5) | data formatting | bytes 64 | tf_op jit(solution)/shard_map/squeeze | solution.py:335
  2.6 50.5 %shard_map.104 = (f32[256,256]{1,0:T(8,128)}, f32[256,256]{1,0:T(8,128)}) custom-call(s32[4,2]{1,0:T(4,128)} %copy.11.offsets, s32[1]{0:T(128)} %bitcast.3.counts, f32[256,256]{1,0:T(8,128)} %object_re.1, f32[256,256]{1,0:T(8,128)} %object_im.1, f32[256,256]{1,0:T(8,128)} %probe_re.1, f32[256,256]{1,0:T(8,128)} %probe_im.1, f32[4,256,256]{2,1,0:T(8,128)} %bitcast.4, ...), custom_call_target="tpu_custom_call" | custom-call | tf_op jit(solution)/shard_map/pallas_call | solution.py:314
  53.2 1.7 %copy.15 = f32[256,256]{1,0:T(8,128)} copy(f32[256,256]{1,0:T(8,128)} %get-tuple-element.4) | data formatting | bytes 524288
  54.8 1.7 %copy.16 = f32[256,256]{1,0:T(8,128)} copy(f32[256,256]{1,0:T(8,128)} %get-tuple-element.5) | data formatting | bytes 524288

commit v2 on v1

--- a/solution.py
+++ b/solution.py
@@ -49,8 +49,9 @@
 
 
 def kernel(
-    rows, cols, offsets, counts, object_re, object_im, probe_re, probe_im, intensity, left, right,
-    out_re, out_im, ext, grad, probes, roots, picked, turned, from_rows, from_cols, send, recv,
+    rows, cols, offsets, counts, object_re, object_im, probe_re, probe_im, stored_i, stored_l, stored_r,
+    out_re, out_im, ext, grad, probes, roots, picked, turned, from_rows, from_cols,
+    intensity, left, right, send, recv, load,
 ):
     width = probe_re.shape[0]
     half = width // 2
@@ -66,12 +67,21 @@
     }
     opposite = {"up": "down", "down": "up", "left": "right", "right": "left"}
 
+    loads = [
+        pltpu.make_async_copy(src, dst, load.at[k])
+        for k, (src, dst) in enumerate(((stored_i, intensity), (stored_l, left), (stored_r, right)))
+    ]
+    for copy in loads:
+        copy.start()
     ext[...] = jnp.zeros_like(ext)
-    from_rows[...] = jnp.zeros_like(from_rows)
-    from_cols[...] = jnp.zeros_like(from_cols)
-    grad[...] = jnp.zeros_like(grad)
     ext[0, inner, inner] = object_re[...].T
     ext[1, inner, inner] = object_im[...].T
+
+    for landing, sides in ((from_rows, ("up", "down")), (from_cols, ("left", "right"))):
+        for k, side in enumerate(sides):
+            @pl.when(jnp.logical_not(there[side][0]))
+            def _(landing=landing, k=k):
+                landing[:, k] = jnp.zeros(landing.shape[:1] + landing.shape[2:], jnp.float32)
 
     barrier = pltpu.get_barrier_semaphore()
     for exists, device in there.values():
@@ -115,6 +125,8 @@
     rightward = Send("right", ext.at[:, half + width - reach : half + width, inner], ext.at[:, lo:half, inner])
     upright = send_rows(half, half + width)
 
+    grad[...] = jnp.zeros_like(grad)
+    loads[0].wait()
     for p in range(slots):
         down_by = lax.rem(offsets[p, 0] + half, width)
         along_by = lax.rem(offsets[p, 1] + half, width)
@@ -133,6 +145,8 @@
                     turned[pl.ds(v, half, stride=2), :]
                 )
 
+    loads[1].wait()
+    loads[2].wait()
     rightward.sent()
     leftward = Send("left", ext.at[:, half : half + reach, inner], ext.at[:, half + width : hi, inner])
     rightward.received()
@@ -295,10 +309,15 @@
     ext[:, half:near, inner] = step(1, half, near, None, from_cols[1, 0, :, 0:reach])
     left_last.received()
     ext[:, far_in : half + width, inner] = step(1, far_in, half + width, None, from_cols[1, 1, :, 0:reach])
-    out_re[...] = ext[0, inner, inner].T
-    out_im[...] = ext[1, inner, inner].T
+    out_re[...] = ext[0, inner, inner]
+    out_im[...] = ext[1, inner, inner]
     for copy in (left_main, left_rest, right_rest, right_main, right_last, left_last):
         copy.sent()
+
+
+def turn(turned_re, turned_im, final_re, final_im):
+    final_re[...] = turned_re[...].T
+    final_im[...] = turned_im[...].T
 
 
 def shards(rows, cols, object_re, object_im, probe_re, probe_im, intensity, offsets, counts):
@@ -311,10 +330,11 @@
     vmem = pl.BlockSpec(memory_space=pltpu.VMEM)
     smem = pl.BlockSpec(memory_space=pltpu.SMEM)
     tile = jax.ShapeDtypeStruct(object_re.shape, f32)
-    return pl.pallas_call(
+    turned = jax.ShapeDtypeStruct(object_re.shape[::-1], f32)
+    turned_re, turned_im = pl.pallas_call(
         functools.partial(kernel, rows, cols),
-        out_shape=(tile, tile),
-        in_specs=[smem, smem] + [vmem] * 7,
+        out_shape=(turned, turned),
+        in_specs=[smem, smem] + [vmem] * 4 + [pl.BlockSpec(memory_space=pl.ANY)] * 3,
         out_specs=(vmem, vmem),
         scratch_shapes=[
             pltpu.VMEM((2, 2 * width, 2 * width), f32),
@@ -325,8 +345,12 @@
             pltpu.VMEM((width, half), f32),
             pltpu.VMEM((ITERS, 2, 2, width + 2 * reach, half), f32),
             pltpu.VMEM((ITERS, 2, 2, 2 * reach, width), f32),
+            pltpu.VMEM(intensity.shape[2:], f32),
+            pltpu.VMEM(left.shape, jnp.bfloat16),
+            pltpu.VMEM(right.shape, jnp.bfloat16),
             pltpu.SemaphoreType.DMA((32,)),
             pltpu.SemaphoreType.DMA((32,)),
+            pltpu.SemaphoreType.DMA((3,)),
         ],
         compiler_params=pltpu.CompilerParams(
             collective_id=0, has_side_effects=True, vmem_limit_bytes=56 * 1024 * 1024
@@ -334,6 +358,9 @@
     )(
         offsets[0, 0], counts[0], object_re, object_im, probe_re, probe_im, intensity[0, 0],
         jnp.asarray(left), jnp.asarray(right),
+    )
+    return pl.pallas_call(turn, out_shape=(tile, tile), in_specs=[vmem] * 2, out_specs=(vmem, vmem))(
+        turned_re, turned_im
     )
 
 

time: 56.7 us -> 53.5 us (0.944)
  local copies, waits for them, and re-layouts: 4.68 us -> 1.34 us
    unnamed x2 -> x0, local copies, waits for them, and re-layouts: 3.34 us -> none
    pallas_call x1 -> x2, Pallas kernels: 50.5 us -> 50.7 us  [the longest x1 48.7 us: shards(): pl.pallas_call(functools.partial(kernel, rows, cols), out_shape=(turned,...]
where the time goes in v2:
time: 53.5 us; the launch traced here: 53.3 us
  Pallas kernels  50.7 us (95%)
  local copies, waits for them, and re-layouts  1.34 us (3%)
  between operations  1.29 us (2%)
    pallas_call x1, Pallas kernels, shards(): pl.pallas_call(functools.partial(kernel, rows, cols), out_shape=(turned,...  48.7 us
    pallas_call x1, Pallas kernels, shards(): pl.pallas_call(turn, out_shape=(tile, tile), in_specs=[vmem] * 2, out_spe...  1.95 us
    squeeze x1, local copies, waits for them, and re-layouts, shards(): offsets[0, 0]  1.34 us

profile of v2, /device:TPU:10, one launch (start us, length us, event | category | flops | bytes accessed | tf_op | source)
XLA Modules:
  0.0 53.3 jit_solution(382577971533182063)
XLA Ops:
  1.3 1.3 %copy.11.offsets = s32[4,2]{1,0:T(4,128)} copy(s32[4,2]{0,1:T(2,128)} %bitcast.5) | data formatting | bytes 64 | tf_op jit(solution)/shard_map/squeeze | solution.py:359
  2.6 48.7 %shard_map.104 = (f32[256,256]{1,0:T(8,128)}, f32[256,256]{1,0:T(8,128)}) custom-call(s32[4,2]{1,0:T(4,128)} %copy.11.offsets, s32[1]{0:T(128)} %bitcast.3.counts, f32[256,256]{1,0:T(8,128)} %object_re.1, f32[256,256]{1,0:T(8,128)} %object_im.1, f32[256,256]{1,0:T(8,128)} %probe_re.1, f32[256,256]{1,0:T(8,128)} %probe_im.1, f32[4,256,256]{2,1,0:T(8,128)} %bitcast.4, ...), custom_call_target="tpu_custom_call" | custom-call | tf_op jit(solution)/shard_map/pallas_call | solution.py:334
  51.4 2.0 %shard_map.105 = (f32[256,256]{1,0:T(8,128)}, f32[256,256]{1,0:T(8,128)}) custom-call(f32[256,256]{1,0:T(8,128)} %get-tuple-element.4.turned_re, f32[256,256]{1,0:T(8,128)} %get-tuple-element.5.turned_im), custom_call_target="tpu_custom_call" | custom-call | tf_op jit(solution)/shard_map/pallas_call | solution.py:362

commit v3 on v2

--- a/solution.py
+++ b/solution.py
@@ -273,10 +273,15 @@
     left_main = start_side(0, "left", lo, split_lo, 0)
     for p in right_slots[1:]:
         visit(0, p)
-    end_rows(0, split_lo, hi, start_rows(0, split_lo, hi))
+    rest_rows = start_rows(0, split_lo, near)
+    edge_rows = start_rows(0, far_in, hi)
+    middle_rows = start_rows(0, near, far_in)
+    end_rows(0, split_lo, near, rest_rows)
     left_rest = start_side(0, "left", split_lo, near, half)
+    end_rows(0, far_in, hi, edge_rows)
     right_rest = start_side(0, "right", far_in + half, hi, half)
     right_main = start_side(0, "right", far_in, far_in + half, 0)
+    end_rows(0, near, far_in, middle_rows)
     leftward.sent()
     left_main.received()
     left_rest.received()
@@ -301,8 +306,11 @@
     right_last = start_side(1, "right", half + width, hi, 0)
     for p in left_slots[1:]:
         visit(1, p)
-    end_rows(1, lo, split_hi, start_rows(1, lo, split_hi))
+    edge_rows = start_rows(1, lo, half)
+    middle_rows = start_rows(1, half, split_hi)
+    end_rows(1, lo, half, edge_rows)
     left_last = start_side(1, "left", lo, half, 0)
+    end_rows(1, half, split_hi, middle_rows)
     for part in (0, 1):
         ext[part, near:far_in, inner] -= step_size * grad[1, part, near:far_in, inner]
     right_last.received()
@@ -348,8 +356,8 @@
             pltpu.VMEM(intensity.shape[2:], f32),
             pltpu.VMEM(left.shape, jnp.bfloat16),
             pltpu.VMEM(right.shape, jnp.bfloat16),
-            pltpu.SemaphoreType.DMA((32,)),
-            pltpu.SemaphoreType.DMA((32,)),
+            pltpu.SemaphoreType.DMA((40,)),
+            pltpu.SemaphoreType.DMA((40,)),
             pltpu.SemaphoreType.DMA((3,)),
         ],
         compiler_params=pltpu.CompilerParams(

time: 53.5 us -> 53.6 us (level)
  no operation moved by 1% of the time
where the time goes in v3:
time: 53.6 us; the launch traced here: 53.5 us
  Pallas kernels  50.8 us (95%)
  local copies, waits for them, and re-layouts  1.34 us (2%)
  between operations  1.29 us (2%)
    pallas_call x1, Pallas kernels, shards(): pl.pallas_call(functools.partial(kernel, rows, cols), out_shape=(turned,...  48.9 us
    pallas_call x1, Pallas kernels, shards(): pl.pallas_call(turn, out_shape=(tile, tile), in_specs=[vmem] * 2, out_spe...  1.95 us
    squeeze x1, local copies, waits for them, and re-layouts, shards(): offsets[0, 0]  1.34 us

profile of v3, /device:TPU:10, one launch (start us, length us, event | category | flops | bytes accessed | tf_op | source)
XLA Modules:
  0.0 53.5 jit_solution(12673349791286114811)
XLA Ops:
  1.3 1.3 %copy.11.offsets = s32[4,2]{1,0:T(4,128)} copy(s32[4,2]{0,1:T(2,128)} %bitcast.5) | data formatting | bytes 64 | tf_op jit(solution)/shard_map/squeeze | solution.py:367
  2.6 48.9 %shard_map.104 = (f32[256,256]{1,0:T(8,128)}, f32[256,256]{1,0:T(8,128)}) custom-call(s32[4,2]{1,0:T(4,128)} %copy.11.offsets, s32[1]{0:T(128)} %bitcast.3.counts, f32[256,256]{1,0:T(8,128)} %object_re.1, f32[256,256]{1,0:T(8,128)} %object_im.1, f32[256,256]{1,0:T(8,128)} %probe_re.1, f32[256,256]{1,0:T(8,128)} %probe_im.1, f32[4,256,256]{2,1,0:T(8,128)} %bitcast.4, ...), custom_call_target="tpu_custom_call" | custom-call | tf_op jit(solution)/shard_map/pallas_call | solution.py:342
  51.5 2.0 %shard_map.105 = (f32[256,256]{1,0:T(8,128)}, f32[256,256]{1,0:T(8,128)}) custom-call(f32[256,256]{1,0:T(8,128)} %get-tuple-element.4.turned_re, f32[256,256]{1,0:T(8,128)} %get-tuple-element.5.turned_im), custom_call_target="tpu_custom_call" | custom-call | tf_op jit(solution)/shard_map/pallas_call | solution.py:370
